TPU v7x, 32 devices: a whole 2x2x4 slice. The times are simulated.
32 devices in a mesh: copies: 2 (over y), sector: 4 (over z), inner: 2 (over x), pair: 2 (over core).
Axes of the slice: x: 2, y: 2, z: 4, core: 2. Of those that a mesh axis runs over, the one named last changes fastest.
Arguments:
- wave_blocks: bfloat16 [8, 512, 512], P(('copies', 'sector'), 'inner'), parts along dimension 0, may hold values from -6 to 6
- left_env: bfloat16 [8, 12, 512, 512], P(('copies', 'sector'), None, 'inner'), parts along dimension 0, may hold values from -0.078125 to 0.078125
- right_env: bfloat16 [8, 12, 512, 512], P(('copies', 'sector'), None, 'pair'), parts along dimension 0, may hold values from -0.25 to 0.25
- source_pairs: int32 [8, 12], P(('copies', 'sector')), parts along dimension 0, may hold values from 0 to 3
- block_sizes: int32 [8], P('copies'), parts along dimension 0, may hold values from 64 to 512, as said below
Outputs:
- sigma_first: bfloat16 [8, 512, 512], P(('copies', 'sector'), 'inner', 'pair'), parts along dimension 0
- sigma_second: bfloat16 [8, 512, 512], P(('copies', 'sector'), 'inner', 'pair'), parts along dimension 0
There are 2 independent parts, one for each index of `copies`. A program takes and returns all parts, laid end to end along the dimension named above; each array names one. Nothing has to cross between parts.
Inputs may be any that keep to these rules, and one draw needn't show every extreme that they name: `block_sizes`: each entry is a multiple of 64.
All inputs are finite; a program needn't handle non-finite values.
Results may differ from a plain program's by a relative error of at most 0.007.
Values may be sent and summed in bfloat16 or wider, within the bound.
A program may use at most 64 MiB of HBM per device.

v0:
```python
import jax
import jax.numpy as jnp
from jax import lax
from jax.sharding import PartitionSpec as P


def body(wave_blocks, left_env, right_env, source_pairs, block_sizes):
    sec_count, row_count, block_width = wave_blocks.shape
    term_count = source_pairs.shape[1]
    col_count = right_env.shape[2]
    first_sector = lax.axis_index("sector") * sec_count
    row_start = lax.axis_index("inner") * row_count
    col_start = lax.axis_index("pair") * col_count
    own_sizes = lax.dynamic_slice_in_dim(block_sizes, first_sector, sec_count, 0)
    row_ids = row_start + jnp.arange(row_count, dtype=jnp.int32)
    col_every = jnp.arange(block_width, dtype=jnp.int32)
    col_ids = col_start + jnp.arange(col_count, dtype=jnp.int32)
    row_live = row_ids[None, :, None] < own_sizes[:, None, None]
    in_mask = row_live & (col_every[None, None, :] < own_sizes[:, None, None])
    out_mask = row_live & (col_ids[None, None, :] < own_sizes[:, None, None])
    masked = jnp.where(in_mask, wave_blocks, jnp.zeros_like(wave_blocks))
    wave_half = lax.dynamic_slice_in_dim(masked, col_start, col_count, 2)
    sources = source_pairs.reshape(-1)
    flat_right = right_env.reshape(sec_count * term_count, col_count, block_width)

    def pick(piece):
        piece_count = piece.shape[0]
        selector = (sources[:, None] == jnp.arange(piece_count, dtype=jnp.int32)[None, :]).astype(
            jnp.bfloat16
        )
        chosen = jnp.einsum("kr,rab->kab", selector, piece, preferred_element_type=jnp.float32)
        return chosen.astype(jnp.bfloat16)

    def contract(source_rows):
        halfway = jnp.einsum(
            "kar,kbr->kab", source_rows, flat_right, preferred_element_type=jnp.float32
        ).astype(jnp.bfloat16)
        halfway = halfway.reshape(sec_count, term_count, row_count, col_count)
        summed = jnp.einsum(
            "skam,skmb->sab",
            left_env,
            lax.all_gather(halfway, "inner", axis=2, tiled=True),
            preferred_element_type=jnp.float32,
        )
        return jnp.where(out_mask, summed, 0.0).astype(jnp.bfloat16)

    def apply_whole(full_rows):
        return contract(pick(lax.all_gather(full_rows, "sector", axis=0, tiled=True)))

    sigma_first = apply_whole(masked)
    wave_wide = wave_half.astype(jnp.float32)
    sigma_wide = sigma_first.astype(jnp.float32)
    entry_total = (
        sec_count * lax.axis_size("sector") * row_count * lax.axis_size("inner") * block_width
    )
    self_norm, correlation_sum, sigma_norm = lax.psum(
        (
            jnp.sum(wave_wide * wave_wide),
            jnp.sum(wave_wide * sigma_wide),
            jnp.sum(sigma_wide * sigma_wide),
        ),
        ("sector", "inner", "pair"),
    )
    rayleigh = correlation_sum / self_norm
    residual = sigma_wide - rayleigh * wave_wide
    residual_sq = sigma_norm - 2.0 * rayleigh * correlation_sum + rayleigh * rayleigh * self_norm
    correction = (residual * lax.rsqrt(residual_sq / entry_total + 1e-06)).astype(jnp.bfloat16)
    full_vector = lax.all_gather(correction, "pair", axis=2, tiled=True)
    sigma_second = apply_whole(full_vector)
    return (sigma_first, sigma_second)


def solution(mesh):
    return jax.shard_map(
        body,
        mesh=mesh,
        in_specs=(
            P(("copies", "sector"), "inner", None),
            P(("copies", "sector"), None, "inner", None),
            P(("copies", "sector"), None, "pair", None),
            P(("copies", "sector"), None),
            P("copies"),
        ),
        out_specs=(
            P(("copies", "sector"), "inner", "pair"),
            P(("copies", "sector"), "inner", "pair"),
        ),
        check_vma=False,
    )
```

profile of v0, /device:TPU:0, one launch (start us, length us, event | category | flops | bytes accessed | tf_op | source)
XLA Modules:
  0.0 226.3 jit_solution(6531152381783769177)
XLA Ops:
  7.2 1.4 dynamic_slice.6
  8.6 0.6 iota_compare_fusion.1
  9.3 0.7 add_compare_fusion.1
  9.9 1.8 copy.10
  11.7 1.1 and_select_fusion
  12.8 0.8 copy.11
  13.7 30.7 %all-gather.7.cloned.1.call-done = bf16[4,256,512]{2,1,0:T(8,128)(2,1)} async-done(((bf16[1,256,512]{2,1,0:T(8,128)(2,1)}), bf16[4,256,512]{2,1,0:T(8,128)(2,1)}) %all-gather.7.cloned.1.call-update) | async-done | bytes 1048592 | tf_op jit(solution)/shard_map/all_gather | solution.py:48
  44.5 2.5 %fusion.37 = bf16[12,256,512]{2,0,1:T(8,128)(2,1)S(1)} fusion(bf16[4,256,512]{2,1,0:T(8,128)(2,1)} %all-gather.7.cloned.1.call-done, s32[12]{0:T(128)} %bitcast.72), kind=kOutput, calls=%fused_computation.21 | convolution fusion | flops 12582960 | bytes 4194352 | tf_op jit(solution)/shard_map/kr,rab->kab/dot_general | solution.py:31
  47.0 3.3 %fusion.11 = bf16[12,256,256]{1,2,0:T(8,128)(2,1)} fusion(bf16[1,12,256,512]{3,2,1,0:T(8,128)(2,1)S(1)} %copy-done, bf16[12,256,512]{2,0,1:T(8,128)(2,1)S(1)} %fusion.37), kind=kOutput, calls=%fused_computation.11 | convolution fusion | flops 806092800 | bytes 7864320 | tf_op jit(solution)/shard_map/kar,kbr->kab/dot_general | solution.py:35
  50.4 0.7 add_compare_fusion
  51.1 43.8 %all-gather.11.cloned.1.call-done = bf16[12,512,256]{1,2,0:T(8,128)(2,1)} async-done(((bf16[12,256,256]{1,2,0:T(8,128)(2,1)}), bf16[12,512,256]{1,2,0:T(8,128)(2,1)}) %all-gather.11.cloned.1.call-update) | async-done | bytes 3145744 | tf_op jit(solution)/shard_map/all_gather | solution.py:42
  94.9 4.5 %fusion.42 = (f32[]{:T(128)}, bf16[256,256]{0,1:T(8,128)(2,1)S(1)}) fusion(bf16[12,512,256]{1,2,0:T(8,128)(2,1)} %all-gather.11.cloned.1.call-done, bf16[1,12,256,512]{3,2,1,0:T(8,128)(2,1)} %param.6, pred[256]{0:T(512)(128)(4,1)S(1)} %add_compare_fusion, pred[256]{0:T(512)(128)(4,1)S(1)} %add_compare_fusion.1), kind=kOutput, calls=%fused_computation.32 | convolution fusion | flops 805699584 | bytes 6423044 | tf_op jit(solution)/shard_map/skam,skmb->sab/dot_general | solution.py:39
  99.4 0.7 fusion.44
  100.1 32.9 %all-reduce = (f32[]{:T(128)}, f32[]{:T(128)}, f32[]{:T(128)}) all-reduce(f32[]{:T(128)} %get-tuple-element.11, f32[]{:T(128)} %get-tuple-element.7, f32[]{:T(128)} %get-tuple-element.6), channel_id=1, replica_groups=mesh['copies'=2,'sector'=4,'inner'=2,'pair'=2] {'sector','inner','pair'}, use_global_device_ids=true, to_apply=%region_5.6 | all-reduce | flops 3 | bytes 24 | tf_op jit(solution)/shard_map/psum | solution.py:56
  136.4 0.1 fusion.41
  136.5 2.0 all_gather.17
  138.5 0.8 copy.12
  139.4 25.3 %all-gather.9.cloned.1.call-done = bf16[4,256,512]{2,1,0:T(8,128)(2,1)} async-done(((bf16[1,256,512]{2,1,0:T(8,128)(2,1)}), bf16[4,256,512]{2,1,0:T(8,128)(2,1)}) %all-gather.9.cloned.1.call-update) | async-done | bytes 1048592 | tf_op jit(solution)/shard_map/all_gather | solution.py:48
  164.7 2.5 %fusion.35 = bf16[12,256,512]{2,0,1:T(8,128)(2,1)S(1)} fusion(bf16[4,256,512]{2,1,0:T(8,128)(2,1)} %all-gather.9.cloned.1.call-done, s32[12]{0:T(128)S(1)} %bitcast.73), kind=kOutput, calls=%fused_computation.19 | convolution fusion | flops 12582960 | bytes 4194352 | tf_op jit(solution)/shard_map/kr,rab->kab/dot_general | solution.py:31
  167.2 3.3 %fusion.8 = bf16[12,256,256]{1,2,0:T(8,128)(2,1)} fusion(bf16[1,12,256,512]{3,2,1,0:T(8,128)(2,1)S(1)} %copy-done, bf16[12,256,512]{2,0,1:T(8,128)(2,1)S(1)} %fusion.35), kind=kOutput, calls=%fused_computation.10 | convolution fusion | flops 806092800 | bytes 7864320 | tf_op jit(solution)/shard_map/kar,kbr->kab/dot_general | solution.py:35
  170.6 0.8 copy.13
  171.3 43.8 %all-gather.13.cloned.1.call-done = bf16[12,512,256]{1,2,0:T(8,128)(2,1)} async-done(((bf16[12,256,256]{1,2,0:T(8,128)(2,1)}), bf16[12,512,256]{1,2,0:T(8,128)(2,1)}) %all-gather.13.cloned.1.call-update) | async-done | bytes 3145744 | tf_op jit(solution)/shard_map/all_gather | solution.py:42
  215.1 3.9 %fusion.32 = bf16[1,256,256]{1,2,0:T(8,128)(2,1)S(1)} fusion(bf16[12,512,256]{1,2,0:T(8,128)(2,1)} %all-gather.13.cloned.1.call-done, bf16[1,12,256,512]{3,2,1,0:T(8,128)(2,1)} %param.6, pred[256]{0:T(512)(128)(4,1)S(1)} %add_compare_fusion.1, pred[256]{0:T(512)(128)(4,1)S(1)} %add_compare_fusion), kind=kOutput, calls=%fused_computation.18 | convolution fusion | flops 805502976 | bytes 6423040 | tf_op jit(solution)/shard_map/skam,skmb->sab/dot_general | solution.py:39
  219.0 0.8 copy.14
  (12 shorter events, 0.2 us)
Async XLA Ops:
  7.2 39.9 %copy-start = (bf16[1,12,256,512]{3,2,1,0:T(8,128)(2,1)S(1)}, bf16[1,12,256,512]{3,2,1,0:T(8,128)(2,1)}, u32[]{:S(2)}) copy-start(bf16[1,12,256,512]{3,2,1,0:T(8,128)(2,1)} %param.7) | copy-start | bytes 9437188
  7.2 37.3 %all-gather.7.cloned.1.call-start = ((), (), s32[]{:S(2)}) async-start(), calls=%async_computation | async-start | bytes 1310720 | tf_op jit(solution)/shard_map/all_gather | solution.py:48
  13.7 81.2 %all-gather.11.cloned.1.call-start = ((), (), s32[]{:S(2)}) async-start(), calls=%async_computation.2 | async-start | bytes 4718592 | tf_op jit(solution)/shard_map/all_gather | solution.py:42
  50.4 114.3 %all-gather.9.cloned.1.call-start = ((), (), s32[]{:S(2)}) async-start(), calls=%async_computation.1 | async-start | bytes 1310720 | tf_op jit(solution)/shard_map/all_gather | solution.py:48
  51.1 113.6 %copy-start.1 = (s32[1,12]{1,0:T(1,128)S(1)}, s32[1,12]{1,0:T(1,128)}, u32[]{:S(2)}) copy-start(s32[1,12]{1,0:T(1,128)} %param.8) | copy-start | bytes 148
  139.4 75.7 %all-gather.13.cloned.1.call-start = ((), (), s32[]{:S(2)}) async-start(), calls=%async_computation.3 | async-start | bytes 4718592 | tf_op jit(solution)/shard_map/all_gather | solution.py:42
Sparse Core Ops, SparseCore 0:
  13.8 30.6 all-gather.6
  50.5 44.3 all-gather.10
  139.5 25.1 all-gather.8
  170.7 44.3 all-gather.12
where the time goes:
time: 227 us; the launch traced here: 226 us
  waiting for transfers between devices  144 us (63%)
  blocking collectives  34.9 us (15%)
  matrix products  20 us (9%)
  between operations  17.3 us (8%)
  local copies, waits for them, and re-layouts  6.38 us (3%)
  other arithmetic  3.83 us (2%)
    all_gather x2, waiting for transfers between devices, contract(): lax.all_gather(halfway, 'inner', axis=2, tiled=True)  87.6 us
    all_gather x2, waiting for transfers between devices, apply_whole(): lax.all_gather(full_rows, 'sector', axis=0, tiled=True)  56 us
    psum x1, blocking collectives, body(): lax.psum((jnp.sum(wave_wide * wave_wide), jnp.sum(wave_wide * sigma_wide)...  32.9 us
    dot_general x2, matrix products, contract(): jnp.einsum('skam,skmb->sab', left_env, lax.all_gather(halfway, 'inner', a...  8.31 us
    dot_general x2, matrix products, contract(): jnp.einsum('kar,kbr->kab', source_rows, flat_right, preferred_element_typ...  6.66 us
    dot_general x2, matrix products, pick(): jnp.einsum('kr,rab->kab', selector, piece, preferred_element_type=jnp.flo...  5.06 us
  transfers between devices with their start and end apart: 4, of which 4 were waited for; matrix products, arithmetic and copies ran while one was open for 1% of the time, Pallas kernels for 0%

commit v1 on v0

v1 whole, which is shorter than its diff:
```python
import functools

import jax
import jax.numpy as jnp
from jax import lax
from jax.experimental import pallas as pl
from jax.experimental.pallas import tpu as pltpu
from jax.sharding import PartitionSpec as P

MESH = pl.DeviceIdType.MESH


def kernel(
    sectors, inners, wave_ref, left_hbm, right_hbm, src_ref, size_ref, first_ref, second_ref,
    field, sigma, left_ref, right_ref, total, load_sem, send_sem, recv_sem,
):
    _, rows, width = wave_ref.shape
    terms, cols = right_ref.shape[0], right_ref.shape[1]
    s = lax.axis_index("sector")
    i = lax.axis_index("inner")
    p = lax.axis_index("pair")
    other = 1 - p
    after = [lax.rem(i + step, inners) for step in range(1, inners)]
    before = [lax.rem(i + inners - step, inners) for step in range(1, inners)]

    loads = (
        pltpu.make_async_copy(left_hbm.at[0], left_ref, load_sem.at[0]),
        pltpu.make_async_copy(right_hbm.at[0], right_ref, load_sem.at[1]),
    )
    for load in loads:
        load.start()

    barrier = pltpu.get_barrier_semaphore()
    for step in range(1, sectors):
        there = lax.rem(s + step, sectors)
        pl.semaphore_signal(barrier, inc=1, device_id={"sector": there}, device_id_type=MESH)
    for there in after:
        pl.semaphore_signal(barrier, inc=1, device_id={"inner": there}, device_id_type=MESH)
    pl.semaphore_signal(barrier, inc=1, device_id={"pair": other}, device_id_type=MESH)

    def part(buffer, half, sector, inner):
        start = pl.multiple_of(inner * rows, rows)
        return buffer.at[half, sector, pl.ds(start, rows), :]

    size = size_ref[s]
    own_row = pl.multiple_of(i * rows, rows)
    row_ids = own_row + lax.broadcasted_iota(jnp.int32, (rows, cols), 0)
    col_ids = lax.broadcasted_iota(jnp.int32, (rows, cols), 1)
    row_live = row_ids < size
    for half in range(width // cols):
        live = row_live & (col_ids + half * cols < size)
        piece = wave_ref[0, :, half * cols:(half + 1) * cols].astype(jnp.float32)
        field[half, s, pl.ds(own_row, rows), :] = jnp.where(live, piece, 0.0).astype(jnp.bfloat16)

    pl.semaphore_wait(barrier, sectors + inners - 1)

    def gather(buffer, phase, share_own):
        started = []

        def send(cond, half, sector, inner, to):
            number = len(started)

            def make():
                ref = part(buffer, half, sector, inner)
                return pltpu.make_async_remote_copy(
                    src_ref=ref, dst_ref=ref, send_sem=send_sem.at[phase, number],
                    recv_sem=recv_sem.at[phase, half, sector, inner],
                    device_id=to, device_id_type=MESH,
                )

            started.append((cond, make))
            make().start()

        def arrive(half, sector, inner):
            ref = part(buffer, half, sector, inner)
            pltpu.make_async_remote_copy(
                src_ref=ref, dst_ref=ref, send_sem=send_sem.at[phase, 0],
                recv_sem=recv_sem.at[phase, half, sector, inner],
                device_id={"pair": other}, device_id_type=MESH,
            ).wait_recv()

        def guarded(cond, work):
            if cond is None:
                work()
            else:
                pl.when(cond)(work)

        def spread(cond, sector):
            for there in after:
                send(cond, p, sector, i, {"inner": there})

        def from_inner(cond, sector):
            def work():
                for there in before:
                    arrive(p, sector, there)
                    send(cond, p, sector, there, {"pair": other})
            guarded(cond, work)

        has_up, has_down = s + 1 < sectors, s >= 1
        up, down = s + 1, s - 1
        pl.when(has_up)(lambda: send(has_up, p, s, i, {"sector": up}))
        pl.when(has_down)(lambda: send(has_down, p, s, i, {"sector": down}))
        spread(None, s)
        if share_own:
            send(None, p, s, i, {"pair": other})

        def from_sector(cond, sector, further, onward):
            both = cond & onward

            def work():
                arrive(p, sector, i)
                pl.when(onward)(lambda: send(both, p, sector, i, {"sector": further}))
                spread(cond, sector)
                send(cond, p, sector, i, {"pair": other})
            guarded(cond, work)

        late = [(None, s)]
        for step in range(1, sectors):
            below, above = s - step >= 0, s + step < sectors
            from_sector(below, s - step, up, has_up)
            from_sector(above, s + step, down, has_down)
            for cond, sector in late:
                from_inner(cond, sector)
            late = [(below, s - step), (above, s + step)]
        for cond, sector in late:
            from_inner(cond, sector)

        for sector in range(sectors):
            for inner in range(inners):
                if share_own:
                    arrive(other, sector, inner)
                else:
                    pl.when((sector != s) | (inner != i))(
                        functools.partial(arrive, other, sector, inner)
                    )
        for cond, make in started:
            guarded(cond, lambda make=make: make().wait_send())

    def dot(a, b, dims):
        return lax.dot_general(a, b, (dims, ((), ())), preferred_element_type=jnp.float32)

    def apply():
        total[...] = jnp.zeros_like(total)

        def term(k, carry):
            source = src_ref[0, k]
            half = sum(
                dot(field[q, source], right_ref[k, :, q * cols:(q + 1) * cols], ((1,), (1,)))
                for q in range(width // cols)
            ).astype(jnp.bfloat16)
            total[...] += dot(left_ref[k], half, ((1,), (0,)))
            return carry

        lax.fori_loop(0, terms, term, 0, unroll=2)
        live = row_live & (col_ids + p * cols < size)
        return jnp.where(live, total[...], 0.0).astype(jnp.bfloat16)

    gather(field, 0, False)
    for load in loads:
        load.wait()
    first = apply()
    first_ref[0] = first
    sigma[p, s, pl.ds(own_row, rows), :] = first
    gather(sigma, 1, True)

    blocks = [(q, t) for q in range(width // cols) for t in range(sectors)]

    def fold(x):
        return jnp.sum(x.reshape(-1, 8, cols), axis=0)

    def sums(n, carry):
        q, t = n // sectors, lax.rem(n, sectors)
        w = field[q, t].astype(jnp.float32)
        g = sigma[q, t].astype(jnp.float32)
        return (carry[0] + fold(w * w), carry[1] + fold(w * g), carry[2] + fold(g * g))

    zero = jnp.zeros((8, cols), jnp.float32)
    self_norm, correlation, sigma_norm = (
        jnp.sum(x) for x in lax.fori_loop(0, len(blocks), sums, (zero, zero, zero))
    )
    self_norm, correlation, sigma_norm = (
        jnp.full((8, cols), x, jnp.float32) for x in (self_norm, correlation, sigma_norm)
    )
    rayleigh = correlation / self_norm
    residual_sq = sigma_norm - 2.0 * rayleigh * correlation + rayleigh * rayleigh * self_norm
    scale = lax.rsqrt(residual_sq / (sectors * width * width) + 1e-06)
    rayleigh, scale = rayleigh[:1], scale[:1]

    def correct(n, carry):
        q, t = n // sectors, lax.rem(n, sectors)
        w = field[q, t].astype(jnp.float32)
        g = sigma[q, t].astype(jnp.float32)
        field[q, t] = ((g - rayleigh * w) * scale).astype(jnp.bfloat16)
        return carry

    lax.fori_loop(0, len(blocks), correct, 0)
    second_ref[0] = apply()


def body(wave_blocks, left_env, right_env, source_pairs, block_sizes):
    _, rows, width = wave_blocks.shape
    terms, cols = right_env.shape[1], right_env.shape[2]
    sectors, inners = lax.axis_size("sector"), lax.axis_size("inner")
    copies = 2 * (sectors + 1) * (inners + 1) + 2 * sectors * inners
    out = jax.ShapeDtypeStruct((1, rows, cols), jnp.bfloat16)
    vmem = pl.BlockSpec(memory_space=pltpu.VMEM)
    smem = pl.BlockSpec(memory_space=pltpu.SMEM)
    hbm = pl.BlockSpec(memory_space=pl.ANY)
    return pl.pallas_call(
        functools.partial(kernel, sectors, inners),
        out_shape=(out, out),
        in_specs=[vmem, hbm, hbm, smem, smem],
        out_specs=(vmem, vmem),
        scratch_shapes=[
            pltpu.VMEM((width // cols, sectors, width, cols), jnp.bfloat16),
            pltpu.VMEM((width // cols, sectors, width, cols), jnp.bfloat16),
            pltpu.VMEM(left_env.shape[1:], jnp.bfloat16),
            pltpu.VMEM(right_env.shape[1:], jnp.bfloat16),
            pltpu.VMEM((rows, cols), jnp.float32),
            pltpu.SemaphoreType.DMA((2,)),
            pltpu.SemaphoreType.DMA((2, copies)),
            pltpu.SemaphoreType.DMA((2, width // cols, sectors, inners)),
        ],
        compiler_params=pltpu.CompilerParams(
            collective_id=0, has_side_effects=True, vmem_limit_bytes=56 * 1024 * 1024
        ),
    )(wave_blocks, left_env, right_env, source_pairs, block_sizes)


def solution(mesh):
    return jax.shard_map(
        body,
        mesh=mesh,
        in_specs=(
            P(("copies", "sector"), "inner", None),
            P(("copies", "sector"), None, "inner", None),
            P(("copies", "sector"), None, "pair", None),
            P(("copies", "sector"), None),
            P("copies"),
        ),
        out_specs=(
            P(("copies", "sector"), "inner", "pair"),
            P(("copies", "sector"), "inner", "pair"),
        ),
        check_vma=False,
    )
```

time: 227 us -> 60.3 us (0.27)
  waiting for transfers between devices: 144 us -> 0 us
  Pallas kernels: 0 us -> 56.3 us
  blocking collectives: 34.9 us -> 0 us
  matrix products: 20 us -> 0 us
  between operations: 17.3 us -> 0.64 us
  other arithmetic: 3.83 us -> 0 us
  local copies, waits for them, and re-layouts: 6.38 us -> 3.14 us
    all_gather x4 -> x0, waiting for transfers between devices: 144 us -> none  [the longest x2 87.6 us: contract(): lax.all_gather(halfway, 'inner', axis=2, tiled=True)]
    pallas_call x0 -> x1, Pallas kernels: none -> 56.3 us  [body(): pl.pallas_call(functools.partial(kernel, sectors, inners), out_shape=(out...]
    psum x1 -> x0, blocking collectives: 32.9 us -> none  [body(): lax.psum((jnp.sum(wave_wide * wave_wide), jnp.sum(wave_wide * sigma_wide)...]
    dot_general x6 -> x0, matrix products: 20 us -> none  [the longest x2 8.31 us: contract(): jnp.einsum('skam,skmb->sab', left_env, lax.all_gather(halfway, 'inner', a...]
  transfers between devices with their start and end apart: 4 -> 0, of which waited for: 4 -> 0; matrix products, arithmetic and copies ran while one was open for 1% -> 0% of each run, Pallas kernels for 0% -> 0%
where the time goes in v1:
time: 60.3 us; the launch traced here: 60.1 us
  Pallas kernels  56.3 us (93%)
  local copies, waits for them, and re-layouts  3.14 us (5%)
  between operations  0.64 us (1%)
    pallas_call x1, Pallas kernels, body(): pl.pallas_call(functools.partial(kernel, sectors, inners), out_shape=(out...  56.3 us
    unnamed x2, local copies, waits for them, and re-layouts  3.14 us

profile of v1, /device:TPU:0, one launch (start us, length us, event | category | flops | bytes accessed | tf_op | source)
XLA Modules:
  0.0 60.1 jit_solution(13455607654974812097)
XLA Ops:
  0.6 56.3 %shard_map.68 = (bf16[1,256,256]{2,1,0:T(8,128)(2,1)}, bf16[1,256,256]{2,1,0:T(8,128)(2,1)}) custom-call(bf16[1,256,512]{2,1,0:T(8,128)(2,1)} %wave_ref.1, bf16[1,12,256,512]{3,2,1,0:T(8,128)(2,1)} %left_hbm.1, bf16[1,12,256,512]{3,2,1,0:T(8,128)(2,1)} %right_hbm.1, s32[1,12]{1,0:T(1,128)} %src_ref.1, s32[4]{0:T(128)} %size_ref.1), custom_call_target="tpu_custom_call" | custom-call | tf_op jit(solution)/shard_map/pallas_call | solution.py:209
  57.0 1.6 %copy.9 = bf16[1,256,256]{2,1,0:T(8,128)(2,1)} copy(bf16[1,256,256]{2,1,0:T(8,128)(2,1)} %get-tuple-element.4) | data formatting | bytes 262144
  58.5 1.6 %copy.10 = bf16[1,256,256]{2,1,0:T(8,128)(2,1)} copy(bf16[1,256,256]{2,1,0:T(8,128)(2,1)} %get-tuple-element.5) | data formatting | bytes 262144

commit v2 on v1

--- a/solution.py
+++ b/solution.py
@@ -11,7 +11,7 @@
 
 
 def kernel(
-    sectors, inners, wave_ref, left_hbm, right_hbm, src_ref, size_ref, first_ref, second_ref,
+    sectors, inners, chunks, wave_ref, left_hbm, right_hbm, src_ref, size_ref, first_ref, second_ref,
     field, sigma, left_ref, right_ref, total, load_sem, send_sem, recv_sem,
 ):
     _, rows, width = wave_ref.shape
@@ -31,16 +31,21 @@
         load.start()
 
     barrier = pltpu.get_barrier_semaphore()
-    for step in range(1, sectors):
-        there = lax.rem(s + step, sectors)
-        pl.semaphore_signal(barrier, inc=1, device_id={"sector": there}, device_id_type=MESH)
+    up, down = s + 1, s - 1
+    has_up, has_down = up < sectors, down >= 0
+    for near, there in ((has_up, up), (has_down, down)):
+        @pl.when(near)
+        def _(there=there):
+            pl.semaphore_signal(barrier, inc=1, device_id={"sector": there}, device_id_type=MESH)
     for there in after:
         pl.semaphore_signal(barrier, inc=1, device_id={"inner": there}, device_id_type=MESH)
     pl.semaphore_signal(barrier, inc=1, device_id={"pair": other}, device_id_type=MESH)
 
-    def part(buffer, half, sector, inner):
-        start = pl.multiple_of(inner * rows, rows)
-        return buffer.at[half, sector, pl.ds(start, rows), :]
+    depth = rows // chunks
+
+    def part(buffer, half, sector, inner, chunk):
+        start = pl.multiple_of(inner * rows + chunk * depth, depth)
+        return buffer.at[half, sector, pl.ds(start, depth), :]
 
     size = size_ref[s]
     own_row = pl.multiple_of(i * rows, rows)
@@ -52,87 +57,87 @@
         piece = wave_ref[0, :, half * cols:(half + 1) * cols].astype(jnp.float32)
         field[half, s, pl.ds(own_row, rows), :] = jnp.where(live, piece, 0.0).astype(jnp.bfloat16)
 
-    pl.semaphore_wait(barrier, sectors + inners - 1)
+    ends = lax.div(s + sectors - 1, sectors) + lax.div(2 * sectors - 2 - s, sectors)
+    pl.semaphore_wait(barrier, inners + ends)
+
+    def guarded(cond, work):
+        if cond is None:
+            work()
+        else:
+            pl.when(cond)(work)
 
     def gather(buffer, phase, share_own):
         started = []
 
-        def send(cond, half, sector, inner, to):
+        def send(cond, half, sector, inner, chunk, to):
             number = len(started)
 
             def make():
-                ref = part(buffer, half, sector, inner)
+                ref = part(buffer, half, sector, inner, chunk)
                 return pltpu.make_async_remote_copy(
                     src_ref=ref, dst_ref=ref, send_sem=send_sem.at[phase, number],
-                    recv_sem=recv_sem.at[phase, half, sector, inner],
+                    recv_sem=recv_sem.at[phase, chunk, half, sector, inner],
                     device_id=to, device_id_type=MESH,
                 )
 
             started.append((cond, make))
             make().start()
 
-        def arrive(half, sector, inner):
-            ref = part(buffer, half, sector, inner)
+        def arrive(half, sector, inner, chunk):
+            ref = part(buffer, half, sector, inner, chunk)
             pltpu.make_async_remote_copy(
                 src_ref=ref, dst_ref=ref, send_sem=send_sem.at[phase, 0],
-                recv_sem=recv_sem.at[phase, half, sector, inner],
+                recv_sem=recv_sem.at[phase, chunk, half, sector, inner],
                 device_id={"pair": other}, device_id_type=MESH,
             ).wait_recv()
 
-        def guarded(cond, work):
-            if cond is None:
-                work()
-            else:
-                pl.when(cond)(work)
-
-        def spread(cond, sector):
+        def spread(cond, sector, chunk):
             for there in after:
-                send(cond, p, sector, i, {"inner": there})
-
-        def from_inner(cond, sector):
+                send(cond, p, sector, i, chunk, {"inner": there})
+
+        def from_inner(cond, sector, chunk):
             def work():
                 for there in before:
-                    arrive(p, sector, there)
-                    send(cond, p, sector, there, {"pair": other})
+                    arrive(p, sector, there, chunk)
+                    send(cond, p, sector, there, chunk, {"pair": other})
             guarded(cond, work)
 
-        has_up, has_down = s + 1 < sectors, s >= 1
-        up, down = s + 1, s - 1
-        pl.when(has_up)(lambda: send(has_up, p, s, i, {"sector": up}))
-        pl.when(has_down)(lambda: send(has_down, p, s, i, {"sector": down}))
-        spread(None, s)
-        if share_own:
-            send(None, p, s, i, {"pair": other})
-
-        def from_sector(cond, sector, further, onward):
+        def from_sector(cond, sector, further, onward, chunk):
             both = cond & onward
 
             def work():
-                arrive(p, sector, i)
-                pl.when(onward)(lambda: send(both, p, sector, i, {"sector": further}))
-                spread(cond, sector)
-                send(cond, p, sector, i, {"pair": other})
+                arrive(p, sector, i, chunk)
+                pl.when(onward)(lambda: send(both, p, sector, i, chunk, {"sector": further}))
+                spread(cond, sector, chunk)
+                send(cond, p, sector, i, chunk, {"pair": other})
             guarded(cond, work)
+
+        for chunk in range(chunks):
+            pl.when(has_up)(lambda: send(has_up, p, s, i, chunk, {"sector": up}))
+            pl.when(has_down)(lambda: send(has_down, p, s, i, chunk, {"sector": down}))
+            spread(None, s, chunk)
+            if share_own:
+                send(None, p, s, i, chunk, {"pair": other})
 
         late = [(None, s)]
         for step in range(1, sectors):
             below, above = s - step >= 0, s + step < sectors
-            from_sector(below, s - step, up, has_up)
-            from_sector(above, s + step, down, has_down)
+            arriving = [(below, s - step), (above, s + step)]
+            for chunk in range(chunks):
+                from_sector(*arriving[0], up, has_up, chunk)
+                from_sector(*arriving[1], down, has_down, chunk)
+                for cond, sector in late:
+                    from_inner(cond, sector, chunk)
+            late = arriving
+        for chunk in range(chunks):
             for cond, sector in late:
-                from_inner(cond, sector)
-            late = [(below, s - step), (above, s + step)]
-        for cond, sector in late:
-            from_inner(cond, sector)
+                from_inner(cond, sector, chunk)
 
         for sector in range(sectors):
             for inner in range(inners):
-                if share_own:
-                    arrive(other, sector, inner)
-                else:
-                    pl.when((sector != s) | (inner != i))(
-                        functools.partial(arrive, other, sector, inner)
-                    )
+                for chunk in range(chunks):
+                    wait = functools.partial(arrive, other, sector, inner, chunk)
+                    guarded(None if share_own else (sector != s) | (inner != i), wait)
         for cond, make in started:
             guarded(cond, lambda make=make: make().wait_send())
 
@@ -151,7 +156,7 @@
             total[...] += dot(left_ref[k], half, ((1,), (0,)))
             return carry
 
-        lax.fori_loop(0, terms, term, 0, unroll=2)
+        lax.fori_loop(0, terms, term, 0, unroll=terms)
         live = row_live & (col_ids + p * cols < size)
         return jnp.where(live, total[...], 0.0).astype(jnp.bfloat16)
 
@@ -201,13 +206,14 @@
     _, rows, width = wave_blocks.shape
     terms, cols = right_env.shape[1], right_env.shape[2]
     sectors, inners = lax.axis_size("sector"), lax.axis_size("inner")
-    copies = 2 * (sectors + 1) * (inners + 1) + 2 * sectors * inners
+    chunks = 2 if sectors * inners <= 16 else 1
+    copies = chunks * (2 * (sectors + 1) * (inners + 1) + 2 * sectors * inners)
     out = jax.ShapeDtypeStruct((1, rows, cols), jnp.bfloat16)
     vmem = pl.BlockSpec(memory_space=pltpu.VMEM)
     smem = pl.BlockSpec(memory_space=pltpu.SMEM)
     hbm = pl.BlockSpec(memory_space=pl.ANY)
     return pl.pallas_call(
-        functools.partial(kernel, sectors, inners),
+        functools.partial(kernel, sectors, inners, chunks),
         out_shape=(out, out),
         in_specs=[vmem, hbm, hbm, smem, smem],
         out_specs=(vmem, vmem),
@@ -219,7 +225,7 @@
             pltpu.VMEM((rows, cols), jnp.float32),
             pltpu.SemaphoreType.DMA((2,)),
             pltpu.SemaphoreType.DMA((2, copies)),
-            pltpu.SemaphoreType.DMA((2, width // cols, sectors, inners)),
+            pltpu.SemaphoreType.DMA((2, chunks, width // cols, sectors, inners)),
         ],
         compiler_params=pltpu.CompilerParams(
             collective_id=0, has_side_effects=True, vmem_limit_bytes=56 * 1024 * 1024

time: 60.3 us -> 52.7 us (0.87)
  Pallas kernels: 56.3 us -> 48.7 us
    pallas_call x1, Pallas kernels: 56.3 us -> 48.7 us  [body(): pl.pallas_call(functools.partial(kernel, sectors, inners, chunks), out_sh...]
where the time goes in v2:
time: 52.7 us; the launch traced here: 52.5 us
  Pallas kernels  48.7 us (92%)
  local copies, waits for them, and re-layouts  3.14 us (6%)
  between operations  0.64 us (1%)
    pallas_call x1, Pallas kernels, body(): pl.pallas_call(functools.partial(kernel, sectors, inners, chunks), out_sh...  48.7 us
    unnamed x2, local copies, waits for them, and re-layouts  3.14 us

profile of v2, /device:TPU:0, one launch (start us, length us, event | category | flops | bytes accessed | tf_op | source)
XLA Modules:
  0.0 52.5 jit_solution(10322058783521534117)
XLA Ops:
  0.6 48.7 %shard_map.68 = (bf16[1,256,256]{2,1,0:T(8,128)(2,1)}, bf16[1,256,256]{2,1,0:T(8,128)(2,1)}) custom-call(bf16[1,256,512]{2,1,0:T(8,128)(2,1)} %wave_ref.1, bf16[1,12,256,512]{3,2,1,0:T(8,128)(2,1)} %left_hbm.1, bf16[1,12,256,512]{3,2,1,0:T(8,128)(2,1)} %right_hbm.1, s32[1,12]{1,0:T(1,128)} %src_ref.1, s32[4]{0:T(128)} %size_ref.1), custom_call_target="tpu_custom_call" | custom-call | tf_op jit(solution)/shard_map/pallas_call | solution.py:215
  49.4 1.6 %copy.9 = bf16[1,256,256]{2,1,0:T(8,128)(2,1)} copy(bf16[1,256,256]{2,1,0:T(8,128)(2,1)} %get-tuple-element.4) | data formatting | bytes 262144
  50.9 1.6 %copy.10 = bf16[1,256,256]{2,1,0:T(8,128)(2,1)} copy(bf16[1,256,256]{2,1,0:T(8,128)(2,1)} %get-tuple-element.5) | data formatting | bytes 262144

commit v3 on v2

--- a/solution.py
+++ b/solution.py
@@ -126,11 +126,9 @@
             for chunk in range(chunks):
                 from_sector(*arriving[0], up, has_up, chunk)
                 from_sector(*arriving[1], down, has_down, chunk)
-                for cond, sector in late:
-                    from_inner(cond, sector, chunk)
-            late = arriving
-        for chunk in range(chunks):
-            for cond, sector in late:
+            late += arriving
+        for cond, sector in late:
+            for chunk in range(chunks):
                 from_inner(cond, sector, chunk)
 
         for sector in range(sectors):
@@ -212,7 +210,7 @@
     vmem = pl.BlockSpec(memory_space=pltpu.VMEM)
     smem = pl.BlockSpec(memory_space=pltpu.SMEM)
     hbm = pl.BlockSpec(memory_space=pl.ANY)
-    return pl.pallas_call(
+    outs = pl.pallas_call(
         functools.partial(kernel, sectors, inners, chunks),
         out_shape=(out, out),
         in_specs=[vmem, hbm, hbm, smem, smem],
@@ -232,6 +230,21 @@
         ),
     )(wave_blocks, left_env, right_env, source_pairs, block_sizes)
 
+    def hand_on(a, b, c, d, sem):
+        moves = [pltpu.make_async_copy(a, c, sem.at[0]), pltpu.make_async_copy(b, d, sem.at[1])]
+        for move in moves:
+            move.start()
+        for move in moves:
+            move.wait()
+
+    return pl.pallas_call(
+        hand_on,
+        out_shape=(out, out),
+        in_specs=[vmem, vmem],
+        out_specs=(hbm, hbm),
+        scratch_shapes=[pltpu.SemaphoreType.DMA((2,))],
+    )(*outs)
+
 
 def solution(mesh):
     return jax.shard_map(

time: 52.7 us -> 49.4 us (0.937)
  local copies, waits for them, and re-layouts: 3.14 us -> 0 us
    unnamed x2 -> x0, local copies, waits for them, and re-layouts: 3.14 us -> none
    pallas_call x1, Pallas kernels: 48.7 us -> 46.9 us  [body(): pl.pallas_call(functools.partial(kernel, sectors, inners, chunks), out_sh...]
    pallas_call x0 -> x1, Pallas kernels: none -> 1.68 us  [body(): pl.pallas_call(hand_on, out_shape=(out, out), in_specs=[vmem, vmem], out_...]
where the time goes in v3:
time: 49.4 us; the launch traced here: 49.2 us
  Pallas kernels  48.6 us (98%)
  between operations  0.64 us (1%)
    pallas_call x1, Pallas kernels, body(): pl.pallas_call(functools.partial(kernel, sectors, inners, chunks), out_sh...  46.9 us
    pallas_call x1, Pallas kernels, body(): pl.pallas_call(hand_on, out_shape=(out, out), in_specs=[vmem, vmem], out_...  1.68 us

profile of v3, /device:TPU:0, one launch (start us, length us, event | category | flops | bytes accessed | tf_op | source)
XLA Modules:
  0.0 49.2 jit_solution(4618386965961806597)
XLA Ops:
  0.6 46.9 %shard_map.68 = (bf16[1,256,256]{2,1,0:T(8,128)(2,1)}, bf16[1,256,256]{2,1,0:T(8,128)(2,1)}) custom-call(bf16[1,256,512]{2,1,0:T(8,128)(2,1)} %wave_ref.1, bf16[1,12,256,512]{3,2,1,0:T(8,128)(2,1)} %left_hbm.1, bf16[1,12,256,512]{3,2,1,0:T(8,128)(2,1)} %right_hbm.1, s32[1,12]{1,0:T(1,128)} %src_ref.1, s32[4]{0:T(128)} %size_ref.1), custom_call_target="tpu_custom_call" | custom-call | tf_op jit(solution)/shard_map/pallas_call | solution.py:213
  47.6 1.7 %shard_map.69 = (bf16[1,256,256]{2,1,0:T(8,128)(2,1)}, bf16[1,256,256]{2,1,0:T(8,128)(2,1)}) custom-call(bf16[1,256,256]{2,1,0:T(8,128)(2,1)} %get-tuple-element.4.a, bf16[1,256,256]{2,1,0:T(8,128)(2,1)} %get-tuple-element.5.b), custom_call_target="tpu_custom_call" | custom-call | tf_op jit(solution)/shard_map/pallas_call | solution.py:240

commit v4 on v3

--- a/solution.py
+++ b/solution.py
@@ -12,7 +12,7 @@
 
 def kernel(
     sectors, inners, chunks, wave_ref, left_hbm, right_hbm, src_ref, size_ref, first_ref, second_ref,
-    field, sigma, left_ref, right_ref, total, load_sem, send_sem, recv_sem,
+    field, sigma, left_ref, right_ref, halfway, load_sem, send_sem, recv_sem,
 ):
     _, rows, width = wave_ref.shape
     terms, cols = right_ref.shape[0], right_ref.shape[1]
@@ -66,7 +66,7 @@
         else:
             pl.when(cond)(work)
 
-    def gather(buffer, phase, share_own):
+    def gather(buffer, phase, share_own, prepare=None):
         started = []
 
         def send(cond, half, sector, inner, chunk, to):
@@ -113,6 +113,8 @@
             guarded(cond, work)
 
         for chunk in range(chunks):
+            if prepare is not None:
+                prepare(chunk)
             pl.when(has_up)(lambda: send(has_up, p, s, i, chunk, {"sector": up}))
             pl.when(has_down)(lambda: send(has_down, p, s, i, chunk, {"sector": down}))
             spread(None, s, chunk)
@@ -136,35 +138,42 @@
                 for chunk in range(chunks):
                     wait = functools.partial(arrive, other, sector, inner, chunk)
                     guarded(None if share_own else (sector != s) | (inner != i), wait)
-        for cond, make in started:
-            guarded(cond, lambda make=make: make().wait_send())
+        def finish():
+            for cond, make in started:
+                guarded(cond, lambda make=make: make().wait_send())
+
+        return finish
 
     def dot(a, b, dims):
         return lax.dot_general(a, b, (dims, ((), ())), preferred_element_type=jnp.float32)
 
-    def apply():
-        total[...] = jnp.zeros_like(total)
-
+    def contract():
         def term(k, carry):
             source = src_ref[0, k]
-            half = sum(
+            halfway[k] = sum(
                 dot(field[q, source], right_ref[k, :, q * cols:(q + 1) * cols], ((1,), (1,)))
                 for q in range(width // cols)
             ).astype(jnp.bfloat16)
-            total[...] += dot(left_ref[k], half, ((1,), (0,)))
             return carry
 
         lax.fori_loop(0, terms, term, 0, unroll=terms)
-        live = row_live & (col_ids + p * cols < size)
-        return jnp.where(live, total[...], 0.0).astype(jnp.bfloat16)
-
-    gather(field, 0, False)
+
+    def finished(chunk):
+        here = slice(chunk * depth, (chunk + 1) * depth)
+        total = sum(dot(left_ref[k, here, :], halfway[k], ((1,), (0,))) for k in range(terms))
+        live = row_live[here] & (col_ids[here] + p * cols < size)
+        return jnp.where(live, total, 0.0).astype(jnp.bfloat16)
+
+    def first_rows(chunk):
+        first = finished(chunk)
+        first_ref[0, chunk * depth:(chunk + 1) * depth, :] = first
+        sigma[p, s, pl.ds(pl.multiple_of(own_row + chunk * depth, depth), depth), :] = first
+
+    field_sent = gather(field, 0, False)
     for load in loads:
         load.wait()
-    first = apply()
-    first_ref[0] = first
-    sigma[p, s, pl.ds(own_row, rows), :] = first
-    gather(sigma, 1, True)
+    contract()
+    sigma_sent = gather(sigma, 1, True, first_rows)
 
     blocks = [(q, t) for q in range(width // cols) for t in range(sectors)]
 
@@ -196,8 +205,12 @@
         field[q, t] = ((g - rayleigh * w) * scale).astype(jnp.bfloat16)
         return carry
 
+    field_sent()
     lax.fori_loop(0, len(blocks), correct, 0)
-    second_ref[0] = apply()
+    contract()
+    for chunk in range(chunks):
+        second_ref[0, chunk * depth:(chunk + 1) * depth, :] = finished(chunk)
+    sigma_sent()
 
 
 def body(wave_blocks, left_env, right_env, source_pairs, block_sizes):
@@ -220,7 +233,7 @@
             pltpu.VMEM((width // cols, sectors, width, cols), jnp.bfloat16),
             pltpu.VMEM(left_env.shape[1:], jnp.bfloat16),
             pltpu.VMEM(right_env.shape[1:], jnp.bfloat16),
-            pltpu.VMEM((rows, cols), jnp.float32),
+            pltpu.VMEM((terms, width, cols), jnp.bfloat16),
             pltpu.SemaphoreType.DMA((2,)),
             pltpu.SemaphoreType.DMA((2, copies)),
             pltpu.SemaphoreType.DMA((2, chunks, width // cols, sectors, inners)),

time: 49.4 us -> 47.7 us (0.966); the launches traced: 49.2 us -> 47 us
  Pallas kernels: 48.6 us -> 46.4 us
    pallas_call x1, Pallas kernels: 46.9 us -> 44.7 us  [body(): pl.pallas_call(functools.partial(kernel, sectors, inners, chunks), out_sh...]
where the time goes in v4:
time: 47.7 us; the launch traced here: 47 us
  Pallas kernels  46.4 us (97%)
  between operations  0.64 us (1%)
    pallas_call x1, Pallas kernels, body(): pl.pallas_call(functools.partial(kernel, sectors, inners, chunks), out_sh...  44.7 us
    pallas_call x1, Pallas kernels, body(): pl.pallas_call(hand_on, out_shape=(out, out), in_specs=[vmem, vmem], out_...  1.68 us

profile of v4, /device:TPU:0, one launch (start us, length us, event | category | flops | bytes accessed | tf_op | source)
XLA Modules:
  0.0 47.0 jit_solution(5578324706615212072)
XLA Ops:
  0.6 44.7 %shard_map.68 = (bf16[1,256,256]{2,1,0:T(8,128)(2,1)}, bf16[1,256,256]{2,1,0:T(8,128)(2,1)}) custom-call(bf16[1,256,512]{2,1,0:T(8,128)(2,1)} %wave_ref.1, bf16[1,12,256,512]{3,2,1,0:T(8,128)(2,1)} %left_hbm.1, bf16[1,12,256,512]{3,2,1,0:T(8,128)(2,1)} %right_hbm.1, s32[1,12]{1,0:T(1,128)} %src_ref.1, s32[4]{0:T(128)} %size_ref.1), custom_call_target="tpu_custom_call" | custom-call | tf_op jit(solution)/shard_map/pallas_call | solution.py:226
  45.3 1.7 %shard_map.69 = (bf16[1,256,256]{2,1,0:T(8,128)(2,1)}, bf16[1,256,256]{2,1,0:T(8,128)(2,1)}) custom-call(bf16[1,256,256]{2,1,0:T(8,128)(2,1)} %get-tuple-element.4.a, bf16[1,256,256]{2,1,0:T(8,128)(2,1)} %get-tuple-element.5.b), custom_call_target="tpu_custom_call" | custom-call | tf_op jit(solution)/shard_map/pallas_call | solution.py:253
